TPU v7x, 128 devices: a whole 4x4x4 slice. The times are simulated.
128 devices in a mesh: ctx: 16 (over y, z), head: 8 (over x, core).
Axes of the slice: x: 4, y: 4, z: 4, core: 2. Of those that a mesh axis runs over, the one named last changes fastest.
Arguments:
- queries: bfloat16 [8192, 5120], P('ctx', 'head'), may hold values from -6 to 6
- key_heads: bfloat16 [8192, 1024], P('ctx', 'head'), may hold values from -6 to 6
- value_heads: bfloat16 [8192, 1024], P('ctx', 'head'), may hold values from -24 to 24
- log_gates: float32 [8192, 8], P('ctx', 'head'), may hold values from -0.75 to 0, as said below
- norm_gain: float32 [5120], P('head'), may hold values from 0.25 to 1.75
- out_weight: bfloat16 [5120, 5120], P('head'), may hold values from -0.125 to 0.125
Outputs:
- layer_out: bfloat16 [5120, 8192], P('head', 'ctx')
Inputs may be any that keep to these rules, and one draw needn't show every extreme that they name: `log_gates`: every entry is negative.
All inputs are finite; a program needn't handle non-finite values.
Results may differ from a plain program's by a relative error of at most 0.017.
Values may be sent and summed in bfloat16 or wider, within the bound.
No kernel may reach another device: no remote copies, remote signals or barrier semaphores. Data moves between devices by JAX's collectives and lax.ppermute only.
A program may use at most 256 MiB of HBM per device.

v0:
```python
import math

import jax
import jax.numpy as jnp
import numpy as np
from jax import lax
from jax.sharding import PartitionSpec as P

HEAD_DIM = 128
GROUP_HEADS = 5
FEATURES = 8256


root_two = math.sqrt(2.0)


def prefix_2(value, axis, join, neutral):
    place = lax.axis_index(axis)
    gathered = jax.tree.map(
        lambda a, kind: lax.all_gather(a.astype(kind), axis), value, (jnp.bfloat16, jnp.bfloat16)
    )
    state = jax.tree.map(lambda a, e: jnp.zeros_like(a) + jnp.asarray(e, a.dtype), value, neutral)

    def one(step, state):
        return join(
            state,
            jax.tree.map(
                lambda a, own: lax.dynamic_index_in_dim(a, step, 0, False).astype(own.dtype),
                gathered,
                value,
            ),
        )

    return lax.fori_loop(0, place, one, state)


def pair_tables(dim_count):
    upper_rows, upper_cols = np.triu_indices(dim_count)
    packed_index = (upper_rows * dim_count + upper_cols).astype(np.int32)
    feature_count = packed_index.shape[0]
    spread_index = np.full((dim_count * dim_count,), feature_count, np.int32)
    spread_index[packed_index] = np.arange(feature_count, dtype=np.int32)
    pair_scale = np.where(np.eye(dim_count, dtype=bool), 1.0, root_two).astype(np.float32)
    return (packed_index, spread_index, pair_scale)


def full_pairs(vectors, pair_scale):
    dim_count = vectors.shape[-1]
    outer = vectors[..., :, None] * pair_scale * vectors[..., None, :]
    return outer.reshape(vectors.shape[:-1] + (dim_count * dim_count,))


def combine_states(earlier, later):
    return (earlier[0] * later[0], later[0] * earlier[1] + later[1])


def per_device(queries, key_heads, value_heads, log_gates, norm_gain, out_weight):
    token_count = queries.shape[0]
    packed_index, spread_index, pair_scale = pair_tables(HEAD_DIM)
    pair_scale = jnp.asarray(pair_scale)
    query_tiles = queries.reshape(token_count, GROUP_HEADS, HEAD_DIM)
    cumulative = jnp.cumsum(log_gates[:, 0])
    block_total = cumulative[-1]
    key_block = min(512, token_count)
    key_steps = token_count // key_block
    to_end = jnp.exp(block_total - cumulative)

    def add_state(running, tiles):
        key_tile, value_tile, scale_tile = tiles
        weighted = (
            full_pairs(key_tile.astype(jnp.float32), pair_scale) * scale_tile[:, None]
        ).astype(jnp.bfloat16)
        product = lax.dot_general(
            weighted, value_tile, (((0,), (0,)), ((), ())), preferred_element_type=jnp.float32
        )
        return (running + product, None)

    full_sum, unused = lax.scan(
        add_state,
        jnp.zeros((HEAD_DIM * HEAD_DIM, HEAD_DIM), jnp.float32),
        (
            key_heads.reshape(key_steps, key_block, HEAD_DIM),
            value_heads.reshape(key_steps, key_block, HEAD_DIM),
            to_end.reshape(key_steps, key_block),
        ),
    )
    local_sum = jnp.take(full_sum, jnp.asarray(packed_index), axis=0)
    query_block = min(128, token_count)
    query_steps = token_count // query_block
    positions = lax.iota(jnp.int32, token_count)
    block_ids = jnp.arange(query_steps, dtype=jnp.int32)

    def within_block(block_index):
        offset = block_index * query_block
        query_tile = lax.dynamic_slice_in_dim(query_tiles, offset, query_block, 0)
        cum_tile = lax.dynamic_slice_in_dim(cumulative, offset, query_block, 0)
        inner = jnp.einsum("tqh,sh->qts", query_tile, key_heads, preferred_element_type=jnp.float32)
        causal = (offset + lax.iota(jnp.int32, query_block))[:, None] >= positions[None, :]
        weight = jnp.where(
            causal, jnp.exp(jnp.minimum(cum_tile[:, None] - cumulative[None, :], 0.0)), 0.0
        )
        scores = (inner * inner * weight[None]).astype(jnp.bfloat16)
        return jnp.einsum("qts,sd->tqd", scores, value_heads, preferred_element_type=jnp.float32)

    decay_prod, prefix = prefix_2(
        (jnp.exp(block_total), local_sum),
        "ctx",
        combine_states,
        (jnp.ones((), jnp.float32), jnp.zeros((FEATURES, HEAD_DIM), jnp.float32)),
    )
    prefix_half = prefix.astype(jnp.bfloat16)
    padded_prefix = jnp.concatenate([prefix_half, jnp.zeros((1, HEAD_DIM), jnp.bfloat16)], axis=0)
    spread_prefix = jnp.take(padded_prefix, jnp.asarray(spread_index), axis=0)
    gain_rows = norm_gain.reshape(GROUP_HEADS, HEAD_DIM)

    def read_block(block_index, within):
        offset = block_index * query_block
        query_tile = lax.dynamic_slice_in_dim(query_tiles, offset, query_block, 0)
        cum_tile = lax.dynamic_slice_in_dim(cumulative, offset, query_block, 0)
        qfeat = (
            full_pairs(query_tile.astype(jnp.float32), pair_scale)
            .astype(jnp.bfloat16)
            .reshape(query_block * GROUP_HEADS, HEAD_DIM * HEAD_DIM)
        )
        carried = jnp.dot(qfeat, spread_prefix, preferred_element_type=jnp.float32)
        carried = (
            carried.reshape(query_block, GROUP_HEADS, HEAD_DIM) * jnp.exp(cum_tile)[:, None, None]
        )
        numerator = carried + within
        normed = (
            numerator
            * lax.rsqrt(jnp.mean(numerator * numerator, axis=-1, keepdims=True) + 1e-06)
            * gain_rows
        )
        return normed.astype(jnp.bfloat16)

    def read_fresh(block_index):
        return read_block(block_index, within_block(block_index))

    normed_all = lax.map(read_fresh, block_ids)
    normed = normed_all.reshape(token_count, GROUP_HEADS * HEAD_DIM)
    return lax.psum_scatter(
        lax.dot_general(
            out_weight, normed, (((0,), (1,)), ((), ())), preferred_element_type=jnp.float32
        ).astype(jnp.bfloat16),
        "head",
        scatter_dimension=0,
        tiled=True,
    )


def solution(mesh):
    return jax.shard_map(
        per_device,
        mesh=mesh,
        in_specs=(
            P("ctx", "head"),
            P("ctx", "head"),
            P("ctx", "head"),
            P("ctx", "head"),
            P("head"),
            P("head", None),
        ),
        out_specs=P("head", "ctx"),
        check_vma=False,
    )
```

profile of v0, /device:TPU:30, one launch (start us, length us, event | category | flops | bytes accessed | tf_op | source)
XLA Modules:
  0.0 1136.6 jit_solution(12217004095141297993)
XLA Ops:
  6.5 1.0 reduce-window.9
  8.4 0.6 subtract_exponential_fusion
  9.1 0.8 pad_clamp_fusion
  9.9 12.1 %mul.149 = f32[512,128,128]{2,1,0:T(8,128)} broadcast(bf16[512,128]{1,0:T(8,128)(2,1)} %param.14), dimensions={0,1} | broadcast | bytes 33685504 | tf_op jit(solution)/shard_map/while/body/eval_jaxpr/mul | solution.py:49
  22.0 11.1 mul.154
  33.1 79.7 %fusion.22 = bf16[16384,128]{1,0:T(8,128)(2,1)} fusion(bf16[512,128]{1,0:T(8,128)(2,1)S(1)} %copy-done.5, f32[64,8,128,128]{3,2,1,0:T(8,128)} %bitcast.105, f32[64,8,128,128]{3,2,1,0:T(8,128)} %bitcast.104, f32[512]{0:T(512)S(1)} %subtract_exponential_fusion, f32[16384]{0:T(1024)S(1)} %copy-done), kind=kOutput, calls=%fused_computation.32 | convolution fusion | flops 2181038080 | bytes 71501824 | tf_op jit(solution)/shard_map/while/body/eval_jaxpr/dot_general | solution.py:73
  112.8 19.1 %gather_fusion = bf16[8256,128]{1,0:T(8,128)(2,1)} fusion(bf16[16384,128]{1,0:T(8,128)(2,1)} %fusion.22, s32[9216]{0:T(1024)S(1)} %pad_clamp_fusion), kind=kCustom, calls=%fused_computation | custom fusion | bytes 4260096 | tf_op jit(solution)/shard_map/jit(_take)/gather | solution.py:87
  133.3 0.8 dynamic-update-slice
  134.0 35.5 %all-reduce.1 = bf16[16]{0:T(256)(128)(2,1)S(1)} all-reduce(bf16[16]{0:T(256)(128)(2,1)S(1)} %dynamic-update-slice), channel_id=1, replica_groups=mesh['ctx'=16,'head'=8] {'ctx'}, use_global_device_ids=true, to_apply=%add.1 | all-reduce | flops 16 | bytes 64
  169.5 0.8 copy.22
  170.6 162.4 %all-gather.3.cloned.1.call-done = bf16[132096,128]{1,0:T(8,128)(2,1)} async-done(((bf16[8256,128]{1,0:T(8,128)(2,1)}), bf16[132096,128]{1,0:T(8,128)(2,1)}) %all-gather.3.cloned.1.call-update) | async-done | bytes 33816592 | tf_op jit(solution)/shard_map/all_gather | solution.py:20
  333.0 2.2 broadcast_in_dim.58
  335.2 68.0 %while.28 = (s32[]{:T(128)}, f32[8256,128]{1,0:T(8,128)}, s32[]{:T(128)}, bf16[16]{0:T(256)(128)(2,1)S(1)}, bf16[16,8256,128]{2,1,0:T(8,128)(2,1)}, /*index=5*/s32[]{:T(128)}, s32[]{:T(128)}, s32[]{:T(128)}) while((s32[]{:T(128)}, f32[8256,128]{1,0:T(8,128)}, s32[]{:T(128)}, bf16[16]{0:T(256)(128)(2,1)S(1)}, bf16[16,8256,128]{2,1,0:T(8,128)(2,1)}, ...), condition=%wide.region_3.4_spmd, body=%wide.region_2.3_spmd.sunk | while | flops 3170310 | bytes 10567821 | solution.py:34
  336.4 4.4 convert_add_fusion.2
  342.1 4.4 convert_add_fusion.2
  346.5 0.6 dynamic_slice.48
  347.8 4.4 convert_add_fusion.2
  352.2 0.6 dynamic_slice.48
  353.4 4.4 convert_add_fusion.2
  357.9 0.6 dynamic_slice.48
  359.1 4.5 convert_add_fusion.2
  363.6 0.6 dynamic_slice.48
  364.8 4.4 convert_add_fusion.2
  369.2 0.6 dynamic_slice.48
  370.4 4.4 convert_add_fusion.2
  374.9 0.6 dynamic_slice.48
  376.1 4.4 convert_add_fusion.2
  380.5 0.6 dynamic_slice.48
  381.8 4.4 convert_add_fusion.2
  386.2 0.6 dynamic_slice.48
  387.4 4.4 convert_add_fusion.2
  393.1 4.4 convert_add_fusion.2
  398.7 4.4 convert_add_fusion.2
  403.2 2.4 convert_element_type.71
  405.7 57.8 %gather_fusion.1 = bf16[16384,128]{1,0:T(8,128)(2,1)} fusion(bf16[8257,128]{1,0:T(8,128)(2,1)S(1)} %concatenate.3, s32[16384]{0:T(1024)S(1)} %broadcast_clamp_fusion), kind=kCustom, calls=%fused_computation.1 | custom fusion | bytes 8454144 | tf_op jit(solution)/shard_map/jit(_take)/gather | solution.py:113
  463.5 6.5 copy.21
  470.1 590.1 %while.29 = (s32[]{:T(128)}, bf16[4,128,5,128]{1,3,2,0:T(8,128)(2,1)S(1)}, s32[4]{0:T(128)S(1)}, bf16[512,5,128]{0,2,1:T(8,128)(2,1)S(1)}, bf16[16384,128]{0,1:T...) while((s32[]{:T(128)}, ...), condition=%wide.region_6.7_spmd.clone.clone, body=%wide.region_4.6_spmd.sunk.clone.clone.sunk | while | flops 2885403392 | bytes 343233728 | solution.py:140
  471.5 13.7 %mul.340 = f32[128,5,128,128]{3,2,0,1:T(8,128)} broadcast(bf16[128,5,128]{2,0,1:T(8,128)(2,1)S(1)} %copy.40), dimensions={0,1,3} | broadcast | bytes 42106880 | tf_op jit(solution)/shard_map/while/body/eval_jaxpr/mul | solution.py:49
  485.2 44.7 %mul.341 = f32[128,5,16384]{2,0,1:T(8,128)} reshape(f32[128,5,128,128]{3,2,0,1:T(8,128)} %mul.340) | data formatting | bytes 83886080 | tf_op jit(solution)/shard_map/while/body/eval_jaxpr/mul | solution.py:49
  529.9 13.9 %mul.342 = f32[128,5,128,128]{3,2,0,1:T(8,128)} broadcast(bf16[128,5,128]{2,0,1:T(8,128)(2,1)S(1)} %copy.40), dimensions={0,1,2} | broadcast | bytes 42106880 | tf_op jit(solution)/shard_map/while/body/eval_jaxpr/mul | solution.py:49
  543.9 44.7 %mul.343 = f32[128,5,16384]{2,0,1:T(8,128)} reshape(f32[128,5,128,128]{3,2,0,1:T(8,128)} %mul.342) | data formatting | bytes 83886080 | tf_op jit(solution)/shard_map/while/body/eval_jaxpr/mul | solution.py:49
  588.7 28.0 %fusion.43 = f32[128,5,128]{0,2,1:T(8,128)S(1)} fusion(bf16[16384,128]{0,1:T(8,128)(2,1)} %get-tuple-element.389, f32[128,5,16384]{2,0,1:T(8,128)} %mul.341, f32[128,5,16384]{2,0,1:T(8,128)} %mul.343, f32[16384]{0:T(1024)S(1)} %get-tuple-element.398, f32[128]{0:T(128)S(1)} %get-tuple-element.329), kind=kOutput, calls=%fused_computation.15.clone.1 | convolution fusion | flops 2715893760 | bytes 88474112 | tf_op jit(solution)/shard_map/while/body/eval_jaxpr/dot_general | solution.py:125
  616.8 0.6 multiply_reduce_fusion.2
  619.1 13.7 %mul.340 = f32[128,5,128,128]{3,2,0,1:T(8,128)} broadcast(bf16[128,5,128]{2,0,1:T(8,128)(2,1)S(1)} %copy.40), dimensions={0,1,3} | broadcast | bytes 42106880 | tf_op jit(solution)/shard_map/while/body/eval_jaxpr/mul | solution.py:49
  632.8 44.7 %mul.341 = f32[128,5,16384]{2,0,1:T(8,128)} reshape(f32[128,5,128,128]{3,2,0,1:T(8,128)} %mul.340) | data formatting | bytes 83886080 | tf_op jit(solution)/shard_map/while/body/eval_jaxpr/mul | solution.py:49
  677.5 13.9 %mul.342 = f32[128,5,128,128]{3,2,0,1:T(8,128)} broadcast(bf16[128,5,128]{2,0,1:T(8,128)(2,1)S(1)} %copy.40), dimensions={0,1,2} | broadcast | bytes 42106880 | tf_op jit(solution)/shard_map/while/body/eval_jaxpr/mul | solution.py:49
  691.4 44.7 %mul.343 = f32[128,5,16384]{2,0,1:T(8,128)} reshape(f32[128,5,128,128]{3,2,0,1:T(8,128)} %mul.342) | data formatting | bytes 83886080 | tf_op jit(solution)/shard_map/while/body/eval_jaxpr/mul | solution.py:49
  736.2 28.0 %fusion.43 = f32[128,5,128]{0,2,1:T(8,128)S(1)} fusion(bf16[16384,128]{0,1:T(8,128)(2,1)} %get-tuple-element.389, f32[128,5,16384]{2,0,1:T(8,128)} %mul.341, f32[128,5,16384]{2,0,1:T(8,128)} %mul.343, f32[16384]{0:T(1024)S(1)} %get-tuple-element.398, f32[128]{0:T(128)S(1)} %get-tuple-element.329), kind=kOutput, calls=%fused_computation.15.clone.1 | convolution fusion | flops 2715893760 | bytes 88474112 | tf_op jit(solution)/shard_map/while/body/eval_jaxpr/dot_general | solution.py:125
  764.3 0.6 multiply_reduce_fusion.2
  766.6 13.7 %mul.340 = f32[128,5,128,128]{3,2,0,1:T(8,128)} broadcast(bf16[128,5,128]{2,0,1:T(8,128)(2,1)S(1)} %copy.40), dimensions={0,1,3} | broadcast | bytes 42106880 | tf_op jit(solution)/shard_map/while/body/eval_jaxpr/mul | solution.py:49
  780.3 44.7 %mul.341 = f32[128,5,16384]{2,0,1:T(8,128)} reshape(f32[128,5,128,128]{3,2,0,1:T(8,128)} %mul.340) | data formatting | bytes 83886080 | tf_op jit(solution)/shard_map/while/body/eval_jaxpr/mul | solution.py:49
  825.0 13.9 %mul.342 = f32[128,5,128,128]{3,2,0,1:T(8,128)} broadcast(bf16[128,5,128]{2,0,1:T(8,128)(2,1)S(1)} %copy.40), dimensions={0,1,2} | broadcast | bytes 42106880 | tf_op jit(solution)/shard_map/while/body/eval_jaxpr/mul | solution.py:49
  838.9 44.7 %mul.343 = f32[128,5,16384]{2,0,1:T(8,128)} reshape(f32[128,5,128,128]{3,2,0,1:T(8,128)} %mul.342) | data formatting | bytes 83886080 | tf_op jit(solution)/shard_map/while/body/eval_jaxpr/mul | solution.py:49
  883.7 28.0 %fusion.43 = f32[128,5,128]{0,2,1:T(8,128)S(1)} fusion(bf16[16384,128]{0,1:T(8,128)(2,1)} %get-tuple-element.389, f32[128,5,16384]{2,0,1:T(8,128)} %mul.341, f32[128,5,16384]{2,0,1:T(8,128)} %mul.343, f32[16384]{0:T(1024)S(1)} %get-tuple-element.398, f32[128]{0:T(128)S(1)} %get-tuple-element.329), kind=kOutput, calls=%fused_computation.15.clone.1 | convolution fusion | flops 2715893760 | bytes 88474112 | tf_op jit(solution)/shard_map/while/body/eval_jaxpr/dot_general | solution.py:125
  911.9 0.6 multiply_reduce_fusion.2
  914.1 13.7 %mul.340 = f32[128,5,128,128]{3,2,0,1:T(8,128)} broadcast(bf16[128,5,128]{2,0,1:T(8,128)(2,1)S(1)} %copy.40), dimensions={0,1,3} | broadcast | bytes 42106880 | tf_op jit(solution)/shard_map/while/body/eval_jaxpr/mul | solution.py:49
  927.8 44.7 %mul.341 = f32[128,5,16384]{2,0,1:T(8,128)} reshape(f32[128,5,128,128]{3,2,0,1:T(8,128)} %mul.340) | data formatting | bytes 83886080 | tf_op jit(solution)/shard_map/while/body/eval_jaxpr/mul | solution.py:49
  972.5 13.9 %mul.342 = f32[128,5,128,128]{3,2,0,1:T(8,128)} broadcast(bf16[128,5,128]{2,0,1:T(8,128)(2,1)S(1)} %copy.40), dimensions={0,1,2} | broadcast | bytes 42106880 | tf_op jit(solution)/shard_map/while/body/eval_jaxpr/mul | solution.py:49
  986.5 44.7 %mul.343 = f32[128,5,16384]{2,0,1:T(8,128)} reshape(f32[128,5,128,128]{3,2,0,1:T(8,128)} %mul.342) | data formatting | bytes 83886080 | tf_op jit(solution)/shard_map/while/body/eval_jaxpr/mul | solution.py:49
  1031.3 28.0 %fusion.43 = f32[128,5,128]{0,2,1:T(8,128)S(1)} fusion(bf16[16384,128]{0,1:T(8,128)(2,1)} %get-tuple-element.389, f32[128,5,16384]{2,0,1:T(8,128)} %mul.341, f32[128,5,16384]{2,0,1:T(8,128)} %mul.343, f32[16384]{0:T(1024)S(1)} %get-tuple-element.398, f32[128]{0:T(128)S(1)} %get-tuple-element.329), kind=kOutput, calls=%fused_computation.15.clone.1 | convolution fusion | flops 2715893760 | bytes 88474112 | tf_op jit(solution)/shard_map/while/body/eval_jaxpr/dot_general | solution.py:125
  1059.4 0.6 multiply_reduce_fusion.2
  1060.7 8.9 fusion.24
  1069.7 7.9 copy.25
  1077.6 52.2 %reduce-scatter.4.cloned.1.call-done = bf16[640,512]{1,0:T(8,128)(2,1)} async-done(((bf16[5120,512]{1,0:T(8,128)(2,1)}), bf16[640,512]{1,0:T(8,128)(2,1)}) %reduce-scatter.4.cloned.1.call-update) | async-done | bytes 655376 | tf_op jit(solution)/shard_map/reduce_scatter | solution.py:142
  (77 shorter events, 9.8 us)
Async XLA Ops:
  6.5 326.5 %all-gather.3.cloned.1.call-start = ((), (), s32[]{:S(2)}) async-start(), calls=%async_computation.1 | async-start | bytes 35930112 | tf_op jit(solution)/shard_map/all_gather | solution.py:20
  7.8 1.2 copy-start.6
  9.9 12.1 %copy-start.3 = (bf16[512,128]{1,0:T(8,128)(2,1)S(1)}, bf16[512,128]{1,0:T(8,128)(2,1)}, u32[]{:S(2)}) copy-start(bf16[512,128]{1,0:T(8,128)(2,1)} %param.14) | copy-start | bytes 393220
  22.0 11.1 copy-start
  22.0 11.1 copy-start.5
  112.8 19.9 %copy-start.11 = (u32[128]{0:T(128)S(1)}, u32[128]{0:T(128)}, u32[]{:S(2)}) copy-start(u32[128]{0:T(128)} %constant.127) | copy-start | bytes 1540
  112.8 57.5 %copy-start.2 = (bf16[512,640]{1,0:T(8,128)(2,1)S(1)}, bf16[512,640]{1,0:T(8,128)(2,1)}, u32[]{:S(2)}) copy-start(bf16[512,640]{1,0:T(8,128)(2,1)} %param.13) | copy-start | bytes 1966084
  112.8 57.8 %copy-start.10 = (s32[16384]{0:T(1024)S(1)}, s32[16384]{0:T(1024)}, u32[]{:S(2)}) copy-start(s32[16384]{0:T(1024)} %constant.124) | copy-start | bytes 196612
  131.9 997.8 %reduce-scatter.4.cloned.1.call-start = ((), (), s32[]{:S(2)}) async-start(), calls=%async_computation.2 | async-start | bytes 5898240 | tf_op jit(solution)/shard_map/reduce_scatter | solution.py:142
  463.5 6.5 copy-start.1
  463.5 6.5 copy-start.4
  463.5 6.5 copy-start.7
  463.5 6.5 copy-start.8
  463.5 6.5 copy-start.9
Sparse Core Ops, SparseCore 0:
  132.1 200.8 all-gather.2
  1077.7 51.9 reduce-scatter.3
where the time goes:
time: 1150 us; the launch traced here: 1140 us
  local copies, waits for them, and re-layouts  599 us (52%)
  waiting for transfers between devices  215 us (19%)
  matrix products  203 us (18%)
  other arithmetic  59.4 us (5%)
  blocking collectives  35.5 us (3%)
  between operations  14.3 us (1%)
    mul x18, local copies, waits for them, and re-layouts, full_pairs(): outer = vectors[..., :, None] * pair_scale * vectors[..., None, :]  491 us
    all_gather x1, waiting for transfers between devices, prefix_2(): lax.all_gather(a.astype(kind), axis)  162 us
    dot_general x4, matrix products, read_block(): carried = jnp.dot(qfeat, spread_prefix, preferred_element_type=jnp.float32)  112 us
    dot_general x1, matrix products, add_state(): lax.dot_general(weighted, value_tile, (((0,), (0,)), ((), ())), preferred...  79.7 us
    gather x1, local copies, waits for them, and re-layouts, per_device(): spread_prefix = jnp.take(padded_prefix, jnp.asarray(spread_index), axis=0)  57.8 us
    add x12, other arithmetic, combine_states(): return (earlier[0] * later[0], later[0] * earlier[1] + later[1])  53.2 us
    reduce_scatter x1, waiting for transfers between devices, per_device(): lax.psum_scatter(lax.dot_general(out_weight, normed, (((0,), (1,)), ((),...  52.2 us
    unnamed x1, blocking collectives  35.5 us
  transfers between devices with their start and end apart: 2, of which 2 were waited for; matrix products, arithmetic and copies ran while one was open for 0% of the time, Pallas kernels for 0%

commit v1 on v0

v1 whole, which is shorter than its diff:
```python
import jax
import jax.numpy as jnp
from jax import lax
from jax.experimental import pallas as pl
from jax.experimental.pallas import tpu as pltpu
from jax.sharding import PartitionSpec as P

HEAD_DIM = 128
GROUP_HEADS = 5
TOK = 512
PAY = TOK + 16
SIDE = 4
CHUNK = 640
BF = jnp.bfloat16
F32 = jnp.float32
VMEM = pl.BlockSpec(memory_space=pltpu.VMEM)

CTX = SIDE * SIDE
CTX_Z = {d: [(i, (i // SIDE) * SIDE + (i + d) % SIDE) for i in range(CTX)] for d in (1, -1, 2)}
CTX_Y = {d: [(i, (i + d * SIDE) % CTX) for i in range(CTX)] for d in (1, -1)}
HEAD_X = {d: [(i, (i + 2 * d) % (2 * SIDE)) for i in range(2 * SIDE)] for d in (1, -1)}
CORE = [(i, i ^ 1) for i in range(2 * SIDE)]


def kernel_call(body, outs, flops, nbytes, scratch=(), **extra):
    return pl.pallas_call(
        body,
        out_shape=outs,
        in_specs=extra.pop("in_specs"),
        out_specs=extra.pop("out_specs", jax.tree.map(lambda _: VMEM, outs)),
        scratch_shapes=list(scratch),
        compiler_params=pltpu.CompilerParams(vmem_limit_bytes=48 * 2**20),
        cost_estimate=pl.CostEstimate(flops=flops, bytes_accessed=nbytes, transcendentals=0),
        **extra,
    )


def shape(dims, kind):
    return jax.ShapeDtypeStruct(dims, kind)


def column(row):
    return jnp.broadcast_to(row, (HEAD_DIM, TOK)).T[:, :1]


def prepare_body(key_ref, value_ref, cum_ref, out_ref):
    cum = column(cum_ref[...])
    total = cum_ref[0:1, TOK - 1 : TOK]
    out_ref[:TOK, :HEAD_DIM] = key_ref[...]
    out_ref[:TOK, HEAD_DIM:] = (value_ref[...].astype(F32) * jnp.exp(total - cum)).astype(BF)
    top = total.astype(BF).astype(F32)
    mid = (total - top).astype(BF).astype(F32)
    low = total - top - mid
    rows = lax.broadcasted_iota(jnp.int32, (16, HEAD_DIM), 0)
    lanes = lax.broadcasted_iota(jnp.int32, (16, HEAD_DIM), 1)
    tile = jnp.where(lanes == 0, top, jnp.where(lanes == 1, mid, jnp.where(lanes == 2, low, 0.0)))
    tile = jnp.where(rows == 0, tile, 0.0)
    out_ref[TOK:, :HEAD_DIM] = tile.astype(BF)
    out_ref[TOK:, HEAD_DIM:] = jnp.zeros((16, HEAD_DIM), BF)


def inner(query, key):
    return lax.dot_general(query, key, (((1,), (1,)), ((), ())), preferred_element_type=F32)


def head_cols(head):
    return slice(head * HEAD_DIM, (head + 1) * HEAD_DIM)


def own_body(query_ref, key_ref, value_ref, cum_ref, out_ref):
    cum_col = column(cum_ref[...])
    half = TOK // 2
    for part in range(2):
        rows = slice(part * half, (part + 1) * half)
        seen = (part + 1) * half
        place = part * half + lax.broadcasted_iota(jnp.int32, (half, seen), 0)
        source = lax.broadcasted_iota(jnp.int32, (half, seen), 1)
        decay = jnp.exp(jnp.minimum(cum_col[rows] - cum_ref[0:1, :seen], 0.0))
        decay = jnp.where(place >= source, decay, 0.0)
        for head in range(GROUP_HEADS):
            scores = inner(query_ref[rows, head_cols(head)], key_ref[:seen, :])
            scores = (scores * scores * decay).astype(BF)
            out_ref[rows, head_cols(head)] = jnp.dot(
                scores, value_ref[:seen, :], preferred_element_type=F32
            )


def total_of(ref, slot):
    tile = ref[slot * PAY + TOK : (slot + 1) * PAY, :HEAD_DIM].astype(F32)
    return jnp.sum(jnp.sum(tile, axis=1, keepdims=True), axis=0, keepdims=True)


def slot_places(place_z):
    return [place_z, (place_z + 3) % SIDE, (place_z + 1) % SIDE, (place_z + 2) % SIDE]


def gated(condition, value):
    return jnp.where(condition, value, jnp.zeros_like(value))


def later_sums(places, totals):
    return [
        sum(gated(places[i] > places[k], totals[i]) for i in range(SIDE) if i != k)
        for k in range(SIDE)
    ]


def add_slots(query_ref, pieces, acc_ref, scaled):
    for first in range(0, len(pieces), 2):
        pair = pieces[first : first + 2]
        keys = []
        for index, (ref, slot, log_decay) in enumerate(pair):
            rows = slice(slot * PAY, slot * PAY + TOK)
            values = ref[rows, HEAD_DIM:].astype(F32) * jnp.exp(log_decay)
            scaled[index * TOK : (index + 1) * TOK, :] = values.astype(BF)
            keys.append(ref[rows, :HEAD_DIM])
        key = jnp.concatenate(keys, axis=0)
        value = scaled[: len(pair) * TOK, :]
        for head in range(GROUP_HEADS):
            scores = inner(query_ref[:, head_cols(head)], key)
            scores = (scores * scores).astype(BF)
            acc_ref[:, head_cols(head)] += jnp.dot(scores, value, preferred_element_type=F32)


def row_body(query_ref, own_ref, back_ref, ahead_ref, far_ref, acc_ref, stat_ref, scaled):
    place_z = lax.axis_index("ctx") % SIDE
    places = slot_places(place_z)
    refs = [own_ref, back_ref, ahead_ref, far_ref]
    totals = [total_of(ref, 0) for ref in refs]
    acc_ref[...] = jnp.zeros_like(acc_ref)
    before = sum(gated(places[k] < place_z, totals[k]) for k in range(1, SIDE))
    stat_ref[...] = jnp.broadcast_to(before, stat_ref.shape)
    for k in range(1, SIDE):
        log_decay = sum(
            gated((places[i] > places[k]) & (places[i] < place_z), totals[i])
            for i in range(1, SIDE)
            if i != k
        )

        @pl.when(places[k] < place_z)
        def _():
            add_slots(query_ref, [(refs[k], 0, log_decay)], acc_ref, scaled)


def near_body(query_ref, back_ref, ahead_ref, stat_ref, acc_in, acc_ref, wrap_ref, out_stat, scaled):
    index = lax.axis_index("ctx")
    place_y, places = index // SIDE, slot_places(index % SIDE)
    before = stat_ref[0:1, 0:1]
    totals = [total_of(back_ref, k) for k in range(SIDE)]
    later = later_sums(places, totals)
    out_stat[...] = jnp.broadcast_to(before + sum(totals), out_stat.shape)
    acc_ref[...] = acc_in[...]

    @pl.when(place_y >= 1)
    def _():
        add_slots(query_ref, [(back_ref, k, before + later[k]) for k in range(SIDE)], acc_ref, scaled)

    wrap_later = later_sums(places, [total_of(ahead_ref, k) for k in range(SIDE)])

    @pl.when(place_y == SIDE - 1)
    def _():
        wrap_ref[...] = jnp.zeros_like(wrap_ref)
        add_slots(query_ref, [(ahead_ref, k, wrap_later[k]) for k in range(SIDE)], wrap_ref, scaled)


def last_body(
    query_ref, low_ref, high_ref, stat_ref, acc_in, wrap_ref, own_ref, cum_ref, gain_ref, out_ref, acc, scaled
):
    index = lax.axis_index("ctx")
    place_y, places = index // SIDE, slot_places(index % SIDE)
    before = stat_ref[0:1, 0:1]
    where = [(low_ref, 0), (low_ref, 1), (high_ref, 0), (high_ref, 1)]
    totals = [total_of(*pair) for pair in where]
    later = later_sums(places, totals)
    acc[...] = acc_in[...]

    @pl.when(place_y == SIDE - 1)
    def _():
        acc[...] += jnp.exp(before + sum(totals)) * wrap_ref[...]

    @pl.when(place_y >= 2)
    def _():
        add_slots(query_ref, [(*where[k], before + later[k]) for k in range(SIDE)], acc, scaled)

    grow = jnp.exp(column(cum_ref[...]))
    for head in range(GROUP_HEADS):
        cols = head_cols(head)
        number = own_ref[:, cols] + grow * acc[:, cols]
        mean = jnp.mean(number * number, axis=-1, keepdims=True)
        out_ref[:, cols] = (number * lax.rsqrt(mean + 1e-06) * gain_ref[0:1, cols]).astype(BF)


def project(normed, weight, flip):
    place = lax.axis_index("head").reshape(1)

    def chunk_of(step, place):
        turn = jnp.where(step == 3, 0, jnp.where(step == 2, 3, 2 - step))
        return ((place[0] >> 1) + turn & 3) * 2 + ((place[0] & 1) ^ flip)

    def body(place_ref, normed_ref, weight_ref, out_ref):
        out_ref[0] = jnp.dot(
            normed_ref[...], weight_ref[...], preferred_element_type=F32
        ).astype(BF)

    return pl.pallas_call(
        body,
        out_shape=shape((SIDE, TOK, CHUNK), BF),
        grid_spec=pltpu.PrefetchScalarGridSpec(
            num_scalar_prefetch=1,
            grid=(SIDE,),
            in_specs=[
                pl.BlockSpec((TOK, CHUNK), lambda i, c: (0, 0)),
                pl.BlockSpec((CHUNK, CHUNK), lambda i, c: (0, chunk_of(i, c))),
            ],
            out_specs=pl.BlockSpec((1, TOK, CHUNK), lambda i, c: (i, 0, 0)),
        ),
        compiler_params=pltpu.CompilerParams(vmem_limit_bytes=48 * 2**20),
        cost_estimate=pl.CostEstimate(
            flops=2 * TOK * CHUNK * CHUNK * SIDE, bytes_accessed=6 * 2**20, transcendentals=0
        ),
    )(place, normed, weight)


def presum_body(mine_ref, other_ref, far_r, far_l, near_r, near_l, hold_r, hold_l, own_ref):
    half = TOK // 2

    def both(chunk, rows):
        return mine_ref[chunk, rows, :].astype(F32) + other_ref[chunk, rows, :].astype(F32)

    low, high = slice(0, half), slice(half, TOK)
    far_r[...] = both(0, low).astype(BF)
    far_l[...] = both(0, high).astype(BF)
    near_r[...] = both(1, high).astype(BF)
    near_l[...] = both(2, low).astype(BF)
    hold_r[...] = both(1, low)
    hold_l[...] = both(2, high)
    own_ref[...] = both(3, slice(0, TOK))


def pass_body(hold_r, far_r, hold_l, far_l, out_r, out_l):
    out_r[...] = (hold_r[...] + far_r[...].astype(F32)).astype(BF)
    out_l[...] = (hold_l[...] + far_l[...].astype(F32)).astype(BF)


def finish_body(own_ref, sum_r, sum_l, near_r, near_l, out_ref):
    half = TOK // 2
    low = own_ref[:half, :] + sum_r[...].astype(F32) + near_l[...].astype(F32)
    high = own_ref[half:, :] + sum_l[...].astype(F32) + near_r[...].astype(F32)
    out_ref[:, :half] = low.T.astype(BF)
    out_ref[:, half:] = high.T.astype(BF)


def per_device(queries, key_heads, value_heads, log_gates, norm_gain, out_weight):
    wide = GROUP_HEADS * HEAD_DIM
    cum = jnp.cumsum(log_gates[:, 0]).reshape(1, TOK)
    payload = kernel_call(
        prepare_body, shape((PAY, 2 * HEAD_DIM), BF), 2**18, 2**19, in_specs=[VMEM] * 3
    )(key_heads, value_heads, cum)
    back, ahead, far = (lax.ppermute(payload, "ctx", CTX_Z[d]) for d in (1, -1, 2))
    block_flops = 4 * TOK * TOK * wide
    own = kernel_call(own_body, shape((TOK, wide), F32), block_flops, 2**21, in_specs=[VMEM] * 4)(
        queries, key_heads, value_heads, cum
    )
    row = jnp.concatenate([payload, back, ahead, far], axis=0)
    row_back, row_ahead = (lax.ppermute(row, "ctx", CTX_Y[d]) for d in (1, -1))
    acc_shape = shape((TOK, wide), F32)
    stat_shape = shape((8, HEAD_DIM), F32)
    scaled = pltpu.VMEM((2 * TOK, HEAD_DIM), BF)
    acc, stat = kernel_call(
        row_body, (acc_shape, stat_shape), 3 * block_flops, 2**21, [scaled], in_specs=[VMEM] * 5
    )(queries, payload, back, ahead, far)
    two = 2 * PAY
    low = lax.ppermute(row_back[:two], "ctx", CTX_Y[1])
    high = lax.ppermute(row_ahead[two:], "ctx", CTX_Y[-1])
    acc, wrap, stat = kernel_call(
        near_body,
        (acc_shape, acc_shape, stat_shape),
        8 * block_flops,
        2**22,
        [scaled],
        in_specs=[VMEM] * 5,
    )(queries, row_back, row_ahead, stat, acc)
    normed = kernel_call(
        last_body,
        shape((TOK, wide), BF),
        4 * block_flops,
        2**22,
        [pltpu.VMEM((TOK, wide), F32), scaled],
        in_specs=[VMEM] * 9,
    )(queries, low, high, stat, acc, wrap, own, cum, norm_gain.reshape(1, wide))

    other = lax.ppermute(project(normed, out_weight, 1), "head", CORE)
    mine = project(normed, out_weight, 0)
    half_bf, half_f32 = shape((TOK // 2, CHUNK), BF), shape((TOK // 2, CHUNK), F32)
    far_r, far_l, near_r, near_l, hold_r, hold_l, own_sum = kernel_call(
        presum_body,
        (half_bf,) * 4 + (half_f32,) * 2 + (shape((TOK, CHUNK), F32),),
        2**21,
        2**23,
        in_specs=[VMEM] * 2,
    )(mine, other)
    far_r = lax.ppermute(far_r, "head", HEAD_X[1])
    far_l = lax.ppermute(far_l, "head", HEAD_X[-1])
    near_r = lax.ppermute(near_r, "head", HEAD_X[1])
    near_l = lax.ppermute(near_l, "head", HEAD_X[-1])
    sum_r, sum_l = kernel_call(pass_body, (half_bf,) * 2, 2**19, 2**21, in_specs=[VMEM] * 4)(
        hold_r, far_r, hold_l, far_l
    )
    sum_r = lax.ppermute(sum_r, "head", HEAD_X[1])
    sum_l = lax.ppermute(sum_l, "head", HEAD_X[-1])
    return kernel_call(finish_body, shape((CHUNK, TOK), BF), 2**20, 2**22, in_specs=[VMEM] * 5)(
        own_sum, sum_r, sum_l, near_r, near_l
    )


def solution(mesh):
    return jax.shard_map(
        per_device,
        mesh=mesh,
        in_specs=(
            P("ctx", "head"),
            P("ctx", "head"),
            P("ctx", "head"),
            P("ctx", "head"),
            P("head"),
            P("head", None),
        ),
        out_specs=P("head", "ctx"),
        check_vma=False,
    )
```

time: 1150 us -> 121 us (0.11)
  the two profiles are of different devices: /device:TPU:30 before, /device:TPU:126 now
where the time goes in v1:
time: 121 us
  waiting for transfers between devices  51 us (42%)
  Pallas kernels  42.2 us (35%)
  starting transfers between devices  16.8 us (14%)
  local copies, waits for them, and re-layouts  8.32 us (7%)
  other arithmetic  2.14 us (2%)
    ppermute x2, waiting for transfers between devices, per_device(): row_back, row_ahead = (lax.ppermute(row, 'ctx', CTX_Y[d]) for d in (1, -1))  20 us
    pallas_call x1, Pallas kernels, per_device(): kernel_call(near_body, (acc_shape, acc_shape, stat_shape), 8 * block_flop...  13.3 us
    ppermute x3, waiting for transfers between devices, per_device(): lax.ppermute(payload, 'ctx', CTX_Z[d])  11.7 us
    pallas_call x2, Pallas kernels, project(): pl.pallas_call(body, out_shape=shape((SIDE, TOK, CHUNK), BF), grid_spec=p...  9.4 us
    pallas_call x1, Pallas kernels, per_device(): kernel_call(last_body, shape((TOK, wide), BF), 4 * block_flops, 2 ** 22,...  8.35 us
    unnamed x20, local copies, waits for them, and re-layouts  8.05 us
    ppermute x1, waiting for transfers between devices, per_device(): far_r = lax.ppermute(far_r, 'head', HEAD_X[1])  6.46 us
    ppermute x1, waiting for transfers between devices, per_device(): sum_r = lax.ppermute(sum_r, 'head', HEAD_X[1])  4.89 us
  transfers between devices with their start and end apart: 14, of which 9 were waited for; matrix products, arithmetic and copies ran while one was open for 0% of the time, Pallas kernels for 20%

profile of v1, /device:TPU:126, one launch (start us, length us, event | category | flops | bytes accessed | tf_op | source)
XLA Modules:
  0.0 120.6 jit_solution(13651177417797567999)
XLA Ops:
  0.0 1.0 reduce-window.9
  1.0 0.1 slice.13
  1.1 0.1 slice_reduce_fusion
  1.2 0.1 broadcast_add_fusion
  1.3 0.0 copy-start.1
  1.3 0.9 copy-done.1
  2.2 0.0 copy-start.3
  2.2 0.9 copy-done.3
  3.1 0.0 copy-start.9
  3.1 0.0 copy-start.2
  3.1 0.0 copy-start.4
  3.1 0.3 shard_map.64.own_ref
  3.4 0.6 collective-permute-start.2
  4.1 0.0 collective-permute-start.1
  4.1 3.2 %collective-permute-start = (bf16[528,256]{1,0:T(8,128)(2,1)S(1)}, bf16[528,256]{1,0:T(8,128)(2,1)S(1)}, u32[]{:S(2)}, u32[]{:S(2)}) collective-permute-start(bf16[528,256]{1,0:T(8,128)(2,1)S(1)} %shard_map.64.own_ref), channel_id=1, source_target_pairs={{0,8},{8,16},{16,24},{24,0},{32,40},{40,48},{48,56},{56,32},{64,72... | collective-permute-start | bytes 811016 | tf_op jit(solution)/shard_map/ppermute | solution.py:259
  7.3 7.1 %collective-permute-done.2.far_ref = bf16[528,256]{1,0:T(8,128)(2,1)S(1)} collective-permute-done((bf16[528,256]{1,0:T(8,128)(2,1)S(1)}, bf16[528,256]{1,0:T(8,128)(2,1)S(1)}, u32[]{:S(2)}, u32[]{:S(2)}) %collective-permute-start.2) | collective-permute-done | bytes 270368 | tf_op jit(solution)/shard_map/ppermute | solution.py:259
  14.4 4.6 %collective-permute-done.1.ahead_ref = bf16[528,256]{1,0:T(8,128)(2,1)S(1)} collective-permute-done((bf16[528,256]{1,0:T(8,128)(2,1)S(1)}, bf16[528,256]{1,0:T(8,128)(2,1)S(1)}, u32[]{:S(2)}, u32[]{:S(2)}) %collective-permute-start.1) | collective-permute-done | bytes 270368 | tf_op jit(solution)/shard_map/ppermute | solution.py:259
  19.0 0.0 collective-permute-done.back_ref
  19.0 1.1 pad_maximum_fusion
  20.1 0.7 collective-permute-start.5
  20.8 2.5 %collective-permute-start.3 = (bf16[2112,256]{1,0:T(8,128)(2,1)}, bf16[2112,256]{1,0:T(8,128)(2,1)S(1)}, u32[]{:S(2)}, u32[]{:S(2)}) collective-permute-start(bf16[2112,256]{1,0:T(8,128)(2,1)} %pad_maximum_fusion), channel_id=1, source_target_pairs={{0,32},{8,40},{16,48},{24,56},{32,64},{40,72},{48,80},{56,88},{64,... | collective-permute-start | bytes 3244040 | tf_op jit(solution)/shard_map/ppermute | solution.py:265
  23.3 0.0 copy-done.9
  23.3 0.0 copy-done.2
  23.3 0.0 copy-done.4
  23.3 0.0 copy-start.5
  23.3 1.1 copy-done.5
  24.4 1.8 %shard_map.67.own_ref = f32[512,640]{1,0:T(8,128)S(1)} custom-call(bf16[512,640]{1,0:T(8,128)(2,1)S(1)} %copy-done.5, bf16[512,128]{1,0:T(8,128)(2,1)S(1)} %copy-done.2, bf16[512,128]{1,0:T(8,128)(2,1)S(1)} %copy-done.4, f32[1,512]{1,0:T(1,128)S(1)} %bitcast.4), custom_call_target="tpu_custom_call" | custom-call | flops 671088640 | bytes 2097152 | tf_op jit(solution)/shard_map/pallas_call | solution.py:261
  26.2 0.0 copy-start.6
  26.2 1.1 copy-done.6
  27.3 20.0 %collective-permute-done.5.ahead_ref = bf16[2112,256]{1,0:T(8,128)(2,1)S(1)} collective-permute-done((bf16[2112,256]{1,0:T(8,128)(2,1)}, bf16[2112,256]{1,0:T(8,128)(2,1)S(1)}, u32[]{:S(2)}, u32[]{:S(2)}) %collective-permute-start.5) | collective-permute-done | bytes 1081376 | tf_op jit(solution)/shard_map/ppermute | solution.py:265
  47.3 0.1 collective-permute-start.6
  47.4 0.0 collective-permute-done.3.back_ref
  47.4 3.3 %collective-permute-start.4 = (bf16[1056,256]{1,0:T(8,128)(2,1)S(1)}, bf16[1056,256]{1,0:T(8,128)(2,1)S(1)}, u32[]{:S(2)}, u32[]{:S(2)}) collective-permute-start(bf16[1056,256]{1,0:T(8,128)(2,1)S(1)} %slice.17), channel_id=1, source_target_pairs={{0,32},{8,40},{16,48},{24,56},{32,64},{40,72},{48,80},{56,88},{64,... | collective-permute-start | bytes 1622024 | tf_op jit(solution)/shard_map/ppermute | solution.py:273
  50.7 4.7 %shard_map.65 = (f32[512,640]{1,0:T(8,128)S(1)}, f32[8,128]{1,0:T(8,128)S(1)}) custom-call(bf16[512,640]{1,0:T(8,128)(2,1)S(1)} %copy-done.5, bf16[528,256]{1,0:T(8,128)(2,1)S(1)} %shard_map.64.own_ref, bf16[528,256]{1,0:T(8,128)(2,1)S(1)} %collective-permute-done.back_ref, bf16[528,256]{1,0:T(8,128)(2,1)S(1)} %collective-permute-done.1.ahead_ref, ...), custom_call_target="tpu_custom_call" | custom-call | flops 2013265920 | bytes 2097152 | tf_op jit(solution)/shard_map/pallas_call | solution.py:269
  55.4 0.0 copy-start.7
  55.4 1.1 copy-done.7
  56.5 13.3 %shard_map.66 = (f32[512,640]{1,0:T(8,128)S(1)}, f32[512,640]{1,0:T(8,128)S(1)}, f32[8,128]{1,0:T(8,128)S(1)}) custom-call(bf16[512,640]{1,0:T(8,128)(2,1)S(1)} %copy-done.5, bf16[2112,256]{1,0:T(8,128)(2,1)S(1)} %collective-permute-done.3.back_ref, bf16[2112,256]{1,0:T(8,128)(2,1)S(1)} %collective-permute-done.5.ahead_ref, ...), custom_call_target="tpu_custom_call" | custom-call | flops 5368709120 | bytes 4194304 | tf_op jit(solution)/shard_map/pallas_call | solution.py:275
  69.8 0.0 collective-permute-done.6.high_ref
  69.8 0.0 collective-permute-done.4.low_ref
  69.8 8.4 %shard_map.68.normed_ref = bf16[512,640]{1,0:T(8,128)(2,1)S(1)} custom-call(bf16[512,640]{1,0:T(8,128)(2,1)S(1)} %copy-done.5, bf16[1056,256]{1,0:T(8,128)(2,1)S(1)} %collective-permute-done.4.low_ref, bf16[1056,256]{1,0:T(8,128)(2,1)S(1)} %collective-permute-done.6.high_ref, f32[8,128]{1,0:T(8,128)S(1)} %get-tuple-element.21.stat_ref, ...), custom_call_target="tpu_custom_call" | custom-call | flops 2684354560 | bytes 4194304 | tf_op jit(solution)/shard_map/pallas_call | solution.py:283
  78.2 4.7 %shard_map.70 = bf16[4,512,640]{2,1,0:T(8,128)(2,1)S(1)} custom-call(s32[1]{0:T(128)} %bitcast.place_ref, bf16[512,640]{1,0:T(8,128)(2,1)S(1)} %shard_map.68.normed_ref, bf16[640,5120]{1,0:T(8,128)(2,1)} %weight_ref.3), custom_call_target="tpu_custom_call" | custom-call | flops 1677721600 | bytes 6291456 | tf_op jit(solution)/shard_map/pallas_call | solution.py:205
  82.9 0.1 collective-permute-start.7
  83.0 4.7 %shard_map.69.mine_ref = bf16[4,512,640]{2,1,0:T(8,128)(2,1)S(1)} custom-call(s32[1]{0:T(128)} %bitcast.place_ref, bf16[512,640]{1,0:T(8,128)(2,1)S(1)} %shard_map.68.normed_ref, bf16[640,5120]{1,0:T(8,128)(2,1)} %weight_ref.3), custom_call_target="tpu_custom_call" | custom-call | flops 1677721600 | bytes 6291456 | tf_op jit(solution)/shard_map/pallas_call | solution.py:205
  87.7 0.0 copy-start
  87.7 1.5 %copy-done = bf16[4,512,640]{2,1,0:T(8,128)(2,1)} copy-done((bf16[4,512,640]{2,1,0:T(8,128)(2,1)}, bf16[4,512,640]{2,1,0:T(8,128)(2,1)S(1)}, u32[]{:S(2)}) %copy-start) | copy-done | bytes 2621464
  89.2 0.0 collective-permute-done.7.other_ref
  89.2 0.0 copy-start.8
  89.2 1.5 %copy-done.8 = bf16[4,512,640]{2,1,0:T(8,128)(2,1)} copy-done((bf16[4,512,640]{2,1,0:T(8,128)(2,1)}, bf16[4,512,640]{2,1,0:T(8,128)(2,1)S(1)}, u32[]{:S(2)}) %copy-start.8) | copy-done | bytes 2621464
  90.7 3.1 %shard_map.71 = (bf16[256,640]{1,0:T(8,128)(2,1)S(1)}, bf16[256,640]{1,0:T(8,128)(2,1)S(1)}, bf16[256,640]{1,0:T(8,128)(2,1)S(1)}, bf16[256,640]{1,0:T(8,128)(2,...) custom-call(bf16[4,512,640]{2,1,0:T(8,128)(2,1)} %copy-done, ...), custom_call_target="tpu_custom_call" | custom-call | flops 2097152 | bytes 8388608 | tf_op jit(solution)/shard_map/pallas_call | solution.py:295
  93.8 0.5 collective-permute-start.8
  94.4 1.6 %collective-permute-start.9 = (bf16[256,640]{1,0:T(8,128)(2,1)S(1)}, bf16[256,640]{1,0:T(8,128)(2,1)S(1)}, u32[]{:S(2)}, u32[]{:S(2)}) collective-permute-start(bf16[256,640]{1,0:T(8,128)(2,1)S(1)} %get-tuple-element.28), channel_id=1, source_target_pairs={{0,6},{1,7},{2,0},{3,1},{4,2},{5,3},{6,4},{7,5},{8,14},{9,15},{10,... | collective-permute-start | bytes 983048 | tf_op jit(solution)/shard_map/ppermute | solution.py:303
  95.9 1.7 %collective-permute-start.12 = (bf16[256,640]{1,0:T(8,128)(2,1)S(1)}, bf16[256,640]{1,0:T(8,128)(2,1)S(1)}, u32[]{:S(2)}, u32[]{:S(2)}) collective-permute-start(bf16[256,640]{1,0:T(8,128)(2,1)S(1)} %get-tuple-element.31), channel_id=1, source_target_pairs={{0,2},{1,3},{2,4},{3,5},{4,6},{5,7},{6,0},{7,1},{8,10},{9,11},{10,... | collective-permute-start | bytes 983048 | tf_op jit(solution)/shard_map/ppermute | solution.py:304
  97.6 0.3 collective-permute-start.13
  97.9 6.5 %collective-permute-done.8.far_r = bf16[256,640]{1,0:T(8,128)(2,1)S(1)} collective-permute-done((bf16[256,640]{1,0:T(8,128)(2,1)S(1)}, bf16[256,640]{1,0:T(8,128)(2,1)S(1)}, u32[]{:S(2)}, u32[]{:S(2)}) %collective-permute-start.8) | collective-permute-done | bytes 327712 | tf_op jit(solution)/shard_map/ppermute | solution.py:302
  104.4 1.7 %collective-permute-done.9.far_l = bf16[256,640]{1,0:T(8,128)(2,1)S(1)} collective-permute-done((bf16[256,640]{1,0:T(8,128)(2,1)S(1)}, bf16[256,640]{1,0:T(8,128)(2,1)S(1)}, u32[]{:S(2)}, u32[]{:S(2)}) %collective-permute-start.9) | collective-permute-done | bytes 327712 | tf_op jit(solution)/shard_map/ppermute | solution.py:303
  106.1 0.1 shard_map.72
  106.2 0.4 collective-permute-start.10
  106.6 1.7 %collective-permute-start.11 = (bf16[256,640]{1,0:T(8,128)(2,1)S(1)}, bf16[256,640]{1,0:T(8,128)(2,1)S(1)}, u32[]{:S(2)}, u32[]{:S(2)}) collective-permute-start(bf16[256,640]{1,0:T(8,128)(2,1)S(1)} %get-tuple-element.30), channel_id=1, source_target_pairs={{0,6},{1,7},{2,0},{3,1},{4,2},{5,3},{6,4},{7,5},{8,14},{9,15},{10,... | collective-permute-start | bytes 983048 | tf_op jit(solution)/shard_map/ppermute | solution.py:310
  108.3 3.1 %collective-permute-done.12.near_r = bf16[256,640]{1,0:T(8,128)(2,1)S(1)} collective-permute-done((bf16[256,640]{1,0:T(8,128)(2,1)S(1)}, bf16[256,640]{1,0:T(8,128)(2,1)S(1)}, u32[]{:S(2)}, u32[]{:S(2)}) %collective-permute-start.12) | collective-permute-done | bytes 327712 | tf_op jit(solution)/shard_map/ppermute | solution.py:304
  111.4 1.7 %collective-permute-done.13.near_l = bf16[256,640]{1,0:T(8,128)(2,1)S(1)} collective-permute-done((bf16[256,640]{1,0:T(8,128)(2,1)S(1)}, bf16[256,640]{1,0:T(8,128)(2,1)S(1)}, u32[]{:S(2)}, u32[]{:S(2)}) %collective-permute-start.13) | collective-permute-done | bytes 327712 | tf_op jit(solution)/shard_map/ppermute | solution.py:305
  113.1 4.9 %collective-permute-done.10.sum_r = bf16[256,640]{1,0:T(8,128)(2,1)S(1)} collective-permute-done((bf16[256,640]{1,0:T(8,128)(2,1)S(1)}, bf16[256,640]{1,0:T(8,128)(2,1)S(1)}, u32[]{:S(2)}, u32[]{:S(2)}) %collective-permute-start.10) | collective-permute-done | bytes 327712 | tf_op jit(solution)/shard_map/ppermute | solution.py:309
  118.0 1.4 %collective-permute-done.11.sum_l = bf16[256,640]{1,0:T(8,128)(2,1)S(1)} collective-permute-done((bf16[256,640]{1,0:T(8,128)(2,1)S(1)}, bf16[256,640]{1,0:T(8,128)(2,1)S(1)}, u32[]{:S(2)}, u32[]{:S(2)}) %collective-permute-start.11) | collective-permute-done | bytes 327712 | tf_op jit(solution)/shard_map/ppermute | solution.py:310
  119.4 1.1 shard_map.73
  (4 shorter events, 0.1 us)
Async XLA Ops:
  1.3 0.9 copy-start.1
  2.2 0.9 copy-start.3
  3.1 20.2 %copy-start.9 = (f32[640]{0:T(1024)S(1)}, f32[640]{0:T(1024)}, u32[]{:S(2)}) copy-start(f32[640]{0:T(1024)} %param.10) | copy-start | bytes 7684
  3.1 20.2 %copy-start.2 = (bf16[512,128]{1,0:T(8,128)(2,1)S(1)}, bf16[512,128]{1,0:T(8,128)(2,1)}, u32[]{:S(2)}) copy-start(bf16[512,128]{1,0:T(8,128)(2,1)} %key_ref.3) | copy-start | bytes 393220
  3.1 20.2 %copy-start.4 = (bf16[512,128]{1,0:T(8,128)(2,1)S(1)}, bf16[512,128]{1,0:T(8,128)(2,1)}, u32[]{:S(2)}) copy-start(bf16[512,128]{1,0:T(8,128)(2,1)} %value_ref.3) | copy-start | bytes 393220
  3.4 11.0 %collective-permute-start.2 = (bf16[528,256]{1,0:T(8,128)(2,1)S(1)}, bf16[528,256]{1,0:T(8,128)(2,1)S(1)}, u32[]{:S(2)}, u32[]{:S(2)}) collective-permute-start(bf16[528,256]{1,0:T(8,128)(2,1)S(1)} %shard_map.64.own_ref), channel_id=1, source_target_pairs={{0,16},{8,24},{16,0},{24,8},{32,48},{40,56},{48,32},{56,40},{64,80... | collective-permute-start | bytes 811016 | tf_op jit(solution)/shard_map/ppermute | solution.py:259
  4.1 14.9 %collective-permute-start.1 = (bf16[528,256]{1,0:T(8,128)(2,1)S(1)}, bf16[528,256]{1,0:T(8,128)(2,1)S(1)}, u32[]{:S(2)}, u32[]{:S(2)}) collective-permute-start(bf16[528,256]{1,0:T(8,128)(2,1)S(1)} %shard_map.64.own_ref), channel_id=1, source_target_pairs={{0,24},{8,0},{16,8},{24,16},{32,56},{40,32},{48,40},{56,48},{64,88... | collective-permute-start | bytes 811016 | tf_op jit(solution)/shard_map/ppermute | solution.py:259
  4.1 14.9 %collective-permute-start = (bf16[528,256]{1,0:T(8,128)(2,1)S(1)}, bf16[528,256]{1,0:T(8,128)(2,1)S(1)}, u32[]{:S(2)}, u32[]{:S(2)}) collective-permute-start(bf16[528,256]{1,0:T(8,128)(2,1)S(1)} %shard_map.64.own_ref), channel_id=1, source_target_pairs={{0,8},{8,16},{16,24},{24,0},{32,40},{40,48},{48,56},{56,32},{64,72... | collective-permute-start | bytes 811016 | tf_op jit(solution)/shard_map/ppermute | solution.py:259
  20.1 27.2 %collective-permute-start.5 = (bf16[2112,256]{1,0:T(8,128)(2,1)}, bf16[2112,256]{1,0:T(8,128)(2,1)S(1)}, u32[]{:S(2)}, u32[]{:S(2)}) collective-permute-start(bf16[2112,256]{1,0:T(8,128)(2,1)} %pad_maximum_fusion), channel_id=1, source_target_pairs={{0,96},{8,104},{16,112},{24,120},{32,0},{40,8},{48,16},{56,24},{64... | collective-permute-start | bytes 3244040 | tf_op jit(solution)/shard_map/ppermute | solution.py:265
  20.8 26.6 %collective-permute-start.3 = (bf16[2112,256]{1,0:T(8,128)(2,1)}, bf16[2112,256]{1,0:T(8,128)(2,1)S(1)}, u32[]{:S(2)}, u32[]{:S(2)}) collective-permute-start(bf16[2112,256]{1,0:T(8,128)(2,1)} %pad_maximum_fusion), channel_id=1, source_target_pairs={{0,32},{8,40},{16,48},{24,56},{32,64},{40,72},{48,80},{56,88},{64,... | collective-permute-start | bytes 3244040 | tf_op jit(solution)/shard_map/ppermute | solution.py:265
  23.3 1.1 copy-start.5
  26.2 1.1 copy-start.6
  47.3 22.5 %collective-permute-start.6 = (bf16[1056,256]{1,0:T(8,128)(2,1)S(1)}, bf16[1056,256]{1,0:T(8,128)(2,1)S(1)}, u32[]{:S(2)}, u32[]{:S(2)}) collective-permute-start(bf16[1056,256]{1,0:T(8,128)(2,1)S(1)} %slice.18), channel_id=1, source_target_pairs={{0,96},{8,104},{16,112},{24,120},{32,0},{40,8},{48,16},{56,24},{64... | collective-permute-start | bytes 1622024 | tf_op jit(solution)/shard_map/ppermute | solution.py:274
  47.4 22.4 %collective-permute-start.4 = (bf16[1056,256]{1,0:T(8,128)(2,1)S(1)}, bf16[1056,256]{1,0:T(8,128)(2,1)S(1)}, u32[]{:S(2)}, u32[]{:S(2)}) collective-permute-start(bf16[1056,256]{1,0:T(8,128)(2,1)S(1)} %slice.17), channel_id=1, source_target_pairs={{0,32},{8,40},{16,48},{24,56},{32,64},{40,72},{48,80},{56,88},{64,... | collective-permute-start | bytes 1622024 | tf_op jit(solution)/shard_map/ppermute | solution.py:273
  55.4 1.1 copy-start.7
  82.9 6.3 %collective-permute-start.7 = (bf16[4,512,640]{2,1,0:T(8,128)(2,1)S(1)}, bf16[4,512,640]{2,1,0:T(8,128)(2,1)S(1)}, u32[]{:S(2)}, u32[]{:S(2)}) collective-permute-start(bf16[4,512,640]{2,1,0:T(8,128)(2,1)S(1)} %shard_map.70), channel_id=1, source_target_pairs={{0,1},{1,0},{2,3},{3,2},{4,5},{5,4},{6,7},{7,6},{8,9},{9,8},{10,11... | collective-permute-start | bytes 7864328 | tf_op jit(solution)/shard_map/ppermute | solution.py:292
  87.7 1.5 %copy-start = (bf16[4,512,640]{2,1,0:T(8,128)(2,1)}, bf16[4,512,640]{2,1,0:T(8,128)(2,1)S(1)}, u32[]{:S(2)}) copy-start(bf16[4,512,640]{2,1,0:T(8,128)(2,1)S(1)} %shard_map.69.mine_ref) | copy-start | bytes 7864324
  89.2 1.5 %copy-start.8 = (bf16[4,512,640]{2,1,0:T(8,128)(2,1)}, bf16[4,512,640]{2,1,0:T(8,128)(2,1)S(1)}, u32[]{:S(2)}) copy-start(bf16[4,512,640]{2,1,0:T(8,128)(2,1)S(1)} %collective-permute-done.7.other_ref) | copy-start | bytes 7864324
  93.8 10.6 %collective-permute-start.8 = (bf16[256,640]{1,0:T(8,128)(2,1)S(1)}, bf16[256,640]{1,0:T(8,128)(2,1)S(1)}, u32[]{:S(2)}, u32[]{:S(2)}) collective-permute-start(bf16[256,640]{1,0:T(8,128)(2,1)S(1)} %get-tuple-element.26), channel_id=1, source_target_pairs={{0,2},{1,3},{2,4},{3,5},{4,6},{5,7},{6,0},{7,1},{8,10},{9,11},{10,... | collective-permute-start | bytes 983048 | tf_op jit(solution)/shard_map/ppermute | solution.py:302
  94.4 11.8 %collective-permute-start.9 = (bf16[256,640]{1,0:T(8,128)(2,1)S(1)}, bf16[256,640]{1,0:T(8,128)(2,1)S(1)}, u32[]{:S(2)}, u32[]{:S(2)}) collective-permute-start(bf16[256,640]{1,0:T(8,128)(2,1)S(1)} %get-tuple-element.28), channel_id=1, source_target_pairs={{0,6},{1,7},{2,0},{3,1},{4,2},{5,3},{6,4},{7,5},{8,14},{9,15},{10,... | collective-permute-start | bytes 983048 | tf_op jit(solution)/shard_map/ppermute | solution.py:303
  95.9 15.5 %collective-permute-start.12 = (bf16[256,640]{1,0:T(8,128)(2,1)S(1)}, bf16[256,640]{1,0:T(8,128)(2,1)S(1)}, u32[]{:S(2)}, u32[]{:S(2)}) collective-permute-start(bf16[256,640]{1,0:T(8,128)(2,1)S(1)} %get-tuple-element.31), channel_id=1, source_target_pairs={{0,2},{1,3},{2,4},{3,5},{4,6},{5,7},{6,0},{7,1},{8,10},{9,11},{10,... | collective-permute-start | bytes 983048 | tf_op jit(solution)/shard_map/ppermute | solution.py:304
  97.6 15.5 %collective-permute-start.13 = (bf16[256,640]{1,0:T(8,128)(2,1)S(1)}, bf16[256,640]{1,0:T(8,128)(2,1)S(1)}, u32[]{:S(2)}, u32[]{:S(2)}) collective-permute-start(bf16[256,640]{1,0:T(8,128)(2,1)S(1)} %get-tuple-element.32), channel_id=1, source_target_pairs={{0,6},{1,7},{2,0},{3,1},{4,2},{5,3},{6,4},{7,5},{8,14},{9,15},{10,... | collective-permute-start | bytes 983048 | tf_op jit(solution)/shard_map/ppermute | solution.py:305
  106.2 11.8 %collective-permute-start.10 = (bf16[256,640]{1,0:T(8,128)(2,1)S(1)}, bf16[256,640]{1,0:T(8,128)(2,1)S(1)}, u32[]{:S(2)}, u32[]{:S(2)}) collective-permute-start(bf16[256,640]{1,0:T(8,128)(2,1)S(1)} %get-tuple-element.29), channel_id=1, source_target_pairs={{0,2},{1,3},{2,4},{3,5},{4,6},{5,7},{6,0},{7,1},{8,10},{9,11},{10,... | collective-permute-start | bytes 983048 | tf_op jit(solution)/shard_map/ppermute | solution.py:309
  106.6 12.8 %collective-permute-start.11 = (bf16[256,640]{1,0:T(8,128)(2,1)S(1)}, bf16[256,640]{1,0:T(8,128)(2,1)S(1)}, u32[]{:S(2)}, u32[]{:S(2)}) collective-permute-start(bf16[256,640]{1,0:T(8,128)(2,1)S(1)} %get-tuple-element.30), channel_id=1, source_target_pairs={{0,6},{1,7},{2,0},{3,1},{4,2},{5,3},{6,4},{7,5},{8,14},{9,15},{10,... | collective-permute-start | bytes 983048 | tf_op jit(solution)/shard_map/ppermute | solution.py:310
